TPU v7x, 256 devices: a whole 4x4x8 slice. The times are simulated.
256 devices in a mesh: section: 8 (over z), dp: 32 (over y, x, core).
Axes of the slice: x: 4, y: 4, z: 8, core: 2. Of those that a mesh axis runs over, the one named last changes fastest.
Arguments:
- acts: bfloat16 [8, 4096, 2560], P('section', 'dp'), may hold values from -48 to 48
- out_grad: bfloat16 [4096, 2560], P('dp'), may hold values from -6 to 6
- tok_count: int32 [32], P('dp'), may hold values from 42 to 128, as said below
- norm_gain: float32 [8, 2560], P('section'), may hold values from 0.25 to 1.75
- w_value: bfloat16 [8, 2560, 512], P('section'), may hold values from -0.125 to 0.125
- w_out: bfloat16 [8, 512, 2560], P('section'), may hold values from -0.25 to 0.25
- err_value: bfloat16 [8, 81920, 512], P('section', 'dp'), may hold values from -0.59765625 to 0.59765625
- err_out: bfloat16 [8, 16384, 2560], P('section', 'dp'), may hold values from -0.59765625 to 0.59765625
- start_q_value: float32 [8, 512, 8], P('section'), may hold values from -5 to 5
- start_q_out: float32 [8, 2560, 8], P('section'), may hold values from -5 to 5
Outputs:
- q_value: float32 [8, 512, 8], P('section')
- q_out: float32 [8, 2560, 8], P('section')
Inputs may be any that keep to these rules, and one draw needn't show every extreme that they name: `tok_count`: in every draw one replica has all 128 slots counting and another exactly 42.
All inputs are finite; a program needn't handle non-finite values.
Results may differ from a plain program's by a relative error of at most 0.03.
Values may be sent and summed in bfloat16 or wider, within the bound.
A program may use at most 64 MiB of HBM per device.

v0:
```python
import jax
import jax.numpy as jnp
from jax import lax
from jax.sharding import PartitionSpec as P

epsilon = 1e-06
highest = lax.Precision.HIGHEST


def shifted(block, axis, distance):
    devices = range(lax.axis_size(axis))
    route = [(i - distance, i) for i in devices if i - distance in devices]
    return lax.ppermute(block, axis, route)


def rms_parts(rows_in):
    widened = rows_in.astype(jnp.float32)
    inv_rms = lax.rsqrt(jnp.mean(widened * widened, axis=-1, keepdims=True) + epsilon)
    return (inv_rms, widened * inv_rms)


def branch_back(incoming, inv_rms, unit_rows, gain_row, w_val, w_proj):
    value_grad = lax.dot_general(
        incoming, w_proj, (((1,), (1,)), ((), ())), preferred_element_type=jnp.float32
    ).astype(jnp.bfloat16)
    norm_grad = lax.dot_general(
        value_grad, w_val, (((1,), (1,)), ((), ())), preferred_element_type=jnp.float32
    )
    scaled = norm_grad * gain_row
    centred = scaled - unit_rows * jnp.mean(scaled * unit_rows, axis=-1, keepdims=True)
    return (incoming.astype(jnp.float32) + inv_rms * centred).astype(jnp.bfloat16)


def contract_rows(left_side, right_side):
    return lax.dot_general(
        left_side,
        right_side,
        (((0,), (0,)), ((), ())),
        precision=highest,
        preferred_element_type=jnp.float32,
    )


def apply_gram(basis_raw, gram_matrix):
    lower_factor = jnp.linalg.cholesky(gram_matrix)
    return jax.scipy.linalg.solve_triangular(lower_factor, basis_raw.T, lower=True).T


def shards(
    acts,
    out_grad,
    tok_count,
    norm_gain,
    w_value,
    w_out,
    err_value,
    err_out,
    start_q_value,
    start_q_out,
):
    act_rows = acts[0]
    gain_row = norm_gain[0]
    w_val = w_value[0]
    w_proj = w_out[0]
    row_count = act_rows.shape[0]
    inv_rms, unit_rows = rms_parts(act_rows)
    normed = (unit_rows * gain_row).astype(jnp.bfloat16)
    live_count = tok_count[0]
    live_mask = (jnp.arange(row_count) < live_count)[:, None]
    top_grad = jnp.where(live_mask, out_grad, jnp.zeros_like(out_grad))
    sections = lax.axis_size("section")
    my_section = lax.axis_index("section")
    section_lag = sections - 1 - my_section
    block_count = 1

    def advance(turn_index, loop_grads):
        sent_block = branch_back(loop_grads, inv_rms, unit_rows, gain_row, w_val, w_proj)
        arrived = shifted(sent_block, "section", -1)
        target = turn_index + 1 - section_lag
        usable = (target >= 0) & (target < block_count) & (my_section < sections - 1)
        return jnp.where(usable, arrived, loop_grads)

    section_grads = lax.fori_loop(0, sections + block_count - 2, advance, top_grad)
    value_grad = lax.dot_general(
        section_grads, w_proj, (((1,), (1,)), ((), ())), preferred_element_type=jnp.float32
    ).astype(jnp.bfloat16)
    values = jnp.dot(normed, w_val, preferred_element_type=jnp.float32).astype(jnp.bfloat16)
    scale_down = live_count.astype(jnp.float32)
    grad_value = lax.dot_general(
        normed, value_grad, (((0,), (0,)), ((), ())), preferred_element_type=jnp.float32
    )
    grad_out = lax.dot_general(
        values, section_grads, (((0,), (0,)), ((), ())), preferred_element_type=jnp.float32
    )
    m_value = grad_value / scale_down + err_value[0].astype(jnp.float32)
    m_out = grad_out / scale_down + err_out[0].astype(jnp.float32)
    p_value = jnp.dot(
        m_value, start_q_value[0], precision=highest, preferred_element_type=jnp.float32
    )
    p_out = jnp.dot(m_out, start_q_out[0], precision=highest, preferred_element_type=jnp.float32)
    total_value, total_out = lax.psum((p_value, p_out), "dp")
    basis_value = apply_gram(total_value, contract_rows(total_value, total_value))
    basis_out = apply_gram(total_out, contract_rows(total_out, total_out))
    q_value, q_out = lax.psum(
        (contract_rows(m_value, basis_value), contract_rows(m_out, basis_out)), "dp"
    )
    return (q_value[None], q_out[None])


def solution(mesh):
    placed = (
        P("section", "dp", None),
        P("dp", None),
        P("dp"),
        P("section", None),
        P("section", None, None),
        P("section", None, None),
        P("section", "dp", None),
        P("section", "dp", None),
        P("section", None, None),
        P("section", None, None),
    )
    return jax.shard_map(
        shards,
        mesh=mesh,
        in_specs=placed,
        out_specs=(P("section", None, None), P("section", None, None)),
        check_vma=False,
    )
```

profile of v0, /device:TPU:1, one launch (start us, length us, event | category | flops | bytes accessed | tf_op | source)
XLA Modules:
  0.0 554.2 jit_solution(2717926864972165849)
XLA Ops:
  8.0 1.3 fusion.2
  10.7 155.3 %while.15 = (s32[]{:T(128)}, bf16[128,2560]{1,0:T(8,128)(2,1)S(1)}, s32[]{:T(128)}, pred[]{:T(512)}, f32[128,1]{0,1:T(1,128)S(1)}, /*index=5*/bf16[512,2560]{1,0...) while((s32[]{:T(128)}, bf16[128,2560]{1,0:T(8,128)(2,1)S(1)}, ...), condition=%wide.region_3.4_spmd, body=%wide.region_1.3_spmd.sunk | while | flops 674430976 | bytes 17072836 | solution.py:83
  10.8 4.5 multiply_reduce_fusion.2
  16.5 1.3 collective-permute-start
  17.8 15.8 %collective-permute-done = bf16[128,2560]{1,0:T(8,128)(2,1)S(1)} collective-permute-done((bf16[128,2560]{1,0:T(8,128)(2,1)}, bf16[128,2560]{1,0:T(8,128)(2,1)S(1)}, u32[]{:S(2)}, u32[]{:S(2)}) %collective-permute-start) | collective-permute-done | bytes 655392 | tf_op jit(solution)/shard_map/while/body/eval_jaxpr/ppermute | solution.py:13
  33.8 4.5 multiply_reduce_fusion.2
  39.5 1.3 collective-permute-start
  40.8 17.9 %collective-permute-done = bf16[128,2560]{1,0:T(8,128)(2,1)S(1)} collective-permute-done((bf16[128,2560]{1,0:T(8,128)(2,1)}, bf16[128,2560]{1,0:T(8,128)(2,1)S(1)}, u32[]{:S(2)}, u32[]{:S(2)}) %collective-permute-start) | collective-permute-done | bytes 655392 | tf_op jit(solution)/shard_map/while/body/eval_jaxpr/ppermute | solution.py:13
  58.9 4.5 multiply_reduce_fusion.2
  64.5 1.3 collective-permute-start
  65.8 15.3 %collective-permute-done = bf16[128,2560]{1,0:T(8,128)(2,1)S(1)} collective-permute-done((bf16[128,2560]{1,0:T(8,128)(2,1)}, bf16[128,2560]{1,0:T(8,128)(2,1)S(1)}, u32[]{:S(2)}, u32[]{:S(2)}) %collective-permute-start) | collective-permute-done | bytes 655392 | tf_op jit(solution)/shard_map/while/body/eval_jaxpr/ppermute | solution.py:13
  81.4 4.5 multiply_reduce_fusion.2
  87.1 1.3 collective-permute-start
  88.4 16.3 %collective-permute-done = bf16[128,2560]{1,0:T(8,128)(2,1)S(1)} collective-permute-done((bf16[128,2560]{1,0:T(8,128)(2,1)}, bf16[128,2560]{1,0:T(8,128)(2,1)S(1)}, u32[]{:S(2)}, u32[]{:S(2)}) %collective-permute-start) | collective-permute-done | bytes 655392 | tf_op jit(solution)/shard_map/while/body/eval_jaxpr/ppermute | solution.py:13
  104.9 4.5 multiply_reduce_fusion.2
  110.6 1.3 collective-permute-start
  111.9 14.1 %collective-permute-done = bf16[128,2560]{1,0:T(8,128)(2,1)S(1)} collective-permute-done((bf16[128,2560]{1,0:T(8,128)(2,1)}, bf16[128,2560]{1,0:T(8,128)(2,1)S(1)}, u32[]{:S(2)}, u32[]{:S(2)}) %collective-permute-start) | collective-permute-done | bytes 655392 | tf_op jit(solution)/shard_map/while/body/eval_jaxpr/ppermute | solution.py:13
  126.3 4.5 multiply_reduce_fusion.2
  131.9 1.3 collective-permute-start
  133.2 13.2 %collective-permute-done = bf16[128,2560]{1,0:T(8,128)(2,1)S(1)} collective-permute-done((bf16[128,2560]{1,0:T(8,128)(2,1)}, bf16[128,2560]{1,0:T(8,128)(2,1)S(1)}, u32[]{:S(2)}, u32[]{:S(2)}) %collective-permute-start) | collective-permute-done | bytes 655392 | tf_op jit(solution)/shard_map/while/body/eval_jaxpr/ppermute | solution.py:13
  146.6 4.5 multiply_reduce_fusion.2
  153.6 12.3 %collective-permute-done = bf16[128,2560]{1,0:T(8,128)(2,1)S(1)} collective-permute-done((bf16[128,2560]{1,0:T(8,128)(2,1)}, bf16[128,2560]{1,0:T(8,128)(2,1)S(1)}, u32[]{:S(2)}, u32[]{:S(2)}) %collective-permute-start) | collective-permute-done | bytes 655392 | tf_op jit(solution)/shard_map/while/body/eval_jaxpr/ppermute | solution.py:13
  166.1 6.8 %convert_add_fusion.1 = f32[2560,512]{1,0:T(8,128)} fusion(bf16[1,2560,512]{2,1,0:T(8,128)(2,1)} %param.19, f32[]{:T(128)S(6)} %convert_element_type.69, bf16[128,2560]{1,0:T(8,128)(2,1)S(1)} %get-tuple-element.215, f32[2560]{0:T(1024)S(1)} %reduce.5, bf16[1,512,2560]{2,1,0:T(8,128)(2,1)} %bitcast.91, bf16[1,128,2560]{2,1,0:T(8,128)(2,1)} %param.13, ...), kind=kOutput, calls=%fused_computation.7 | convolution fusion | flops 676397056 | bytes 11807236 | tf_op jit(solution)/shard_map/dot_general | solution.py:89
  172.9 7.7 %fusion.15 = f32[2560,8]{0,1:T(8,128)} fusion(f32[2560,512]{1,0:T(8,128)} %convert_add_fusion.1, f32[1,512,8]{1,2,0:T(8,128)S(1)} %copy-done.4), kind=kOutput, calls=%fused_computation.27 | convolution fusion | flops 125829120 | bytes 5341184 | tf_op jit(solution)/shard_map/dot_general | solution.py:97
  180.9 5.7 %convert_add_fusion = f32[512,2560]{1,0:T(8,128)} fusion(bf16[128,2560]{1,0:T(8,128)(2,1)S(1)} %get-tuple-element.215, bf16[1,512,2560]{2,1,0:T(8,128)(2,1)} %param.20, f32[]{:T(128)S(6)} %convert_element_type.69, bf16[1,128,2560]{2,1,0:T(8,128)(2,1)} %param.13, f32[2560]{0:T(1024)S(1)} %reduce.5, f32[128]{0:T(128)S(1)} %get-tuple-element.238, ...), kind=kOutput, calls=%fused_computation.6 | convolution fusion | flops 676397056 | bytes 11807236 | tf_op jit(solution)/shard_map/dot_general | solution.py:92
  186.6 6.9 %fusion.13 = f32[512,8]{0,1:T(8,128)S(1)} fusion(f32[512,2560]{1,0:T(8,128)} %convert_add_fusion, f32[1,2560,8]{1,2,0:T(8,128)S(1)} %copy-done), kind=kOutput, calls=%fused_computation.25 | convolution fusion | flops 125829120 | bytes 5341184 | tf_op jit(solution)/shard_map/dot_general | solution.py:100
  193.5 102.7 %all-reduce.4.cloned.1.call-done = f32[2560,8]{0,1:T(8,128)} async-done(((f32[2560,8]{0,1:T(8,128)}), f32[2560,8]{0,1:T(8,128)}) %all-reduce.4.cloned.1.call-update) | async-done | bytes 81936 | tf_op jit(solution)/shard_map/psum | solution.py:101
  301.5 5.3 convolution_bitcast_fusion.1
  306.7 121.1 %all-reduce = (f32[1,512,8]{1,2,0:T(8,128)}, f32[512,8]{0,1:T(8,128)S(1)}) all-reduce(f32[1,512,8]{1,2,0:T(8,128)S(1)} %convolution_bitcast_fusion.1, f32[512,8]{0,1:T(8,128)S(1)} %fusion.13), channel_id=1, replica_groups=mesh['section'=8,'dp'=32] {'dp'}, use_global_device_ids=true, to_apply=%region_7.9 | all-reduce | flops 8192 | bytes 65536 | tf_op jit(solution)/shard_map/psum | solution.py:104
  430.9 5.9 %convolution_bitcast_fusion = f32[1,2560,8]{1,2,0:T(8,128)} fusion(f32[512,2560]{1,0:T(8,128)} %convert_add_fusion, f32[8,512]{1,0:T(8,128)S(1)} %fusion.19), kind=kOutput, calls=%fused_computation.8 | convolution fusion | flops 125829120 | bytes 5341184 | tf_op jit(solution)/shard_map/dot_general | solution.py:35
  436.9 109.0 %all-reduce.6.cloned.1.call-done = f32[1,2560,8]{1,2,0:T(8,128)} async-done(((f32[1,2560,8]{1,2,0:T(8,128)}), f32[1,2560,8]{1,2,0:T(8,128)}) %all-reduce.6.cloned.1.call-update) | async-done | bytes 81936 | tf_op jit(solution)/shard_map/psum | solution.py:104
  545.8 1.5 copy.25
  (66 shorter events, 21.2 us)
Async XLA Ops:
  7.2 179.4 %copy-start = (f32[1,2560,8]{1,2,0:T(8,128)S(1)}, f32[1,2560,8]{1,2,0:T(8,128)}, u32[]{:S(2)}) copy-start(f32[1,2560,8]{1,2,0:T(8,128)} %param.22) | copy-start | bytes 245764
  7.2 3.4 copy-start.3
  7.2 3.4 copy-start.2
  7.2 289.1 %all-reduce.4.cloned.1.call-start = ((), (), s32[]{:S(2)}) async-start(), calls=%async_computation | async-start | bytes 163840 | tf_op jit(solution)/shard_map/psum | solution.py:101
  16.5 17.1 %collective-permute-start = (bf16[128,2560]{1,0:T(8,128)(2,1)}, bf16[128,2560]{1,0:T(8,128)(2,1)S(1)}, u32[]{:S(2)}, u32[]{:S(2)}) collective-permute-start(bf16[128,2560]{1,0:T(8,128)(2,1)} %add_convert_fusion.2), channel_id=1, source_target_pairs={{32,0},{64,32},{96,64},{128,96},{160,128},{192,160},{224,192},{33,... | collective-permute-start | bytes 1966088 | tf_op jit(solution)/shard_map/while/body/eval_jaxpr/ppermute | solution.py:13
  39.5 19.2 %collective-permute-start = (bf16[128,2560]{1,0:T(8,128)(2,1)}, bf16[128,2560]{1,0:T(8,128)(2,1)S(1)}, u32[]{:S(2)}, u32[]{:S(2)}) collective-permute-start(bf16[128,2560]{1,0:T(8,128)(2,1)} %add_convert_fusion.2), channel_id=1, source_target_pairs={{32,0},{64,32},{96,64},{128,96},{160,128},{192,160},{224,192},{33,... | collective-permute-start | bytes 1966088 | tf_op jit(solution)/shard_map/while/body/eval_jaxpr/ppermute | solution.py:13
  64.5 16.6 %collective-permute-start = (bf16[128,2560]{1,0:T(8,128)(2,1)}, bf16[128,2560]{1,0:T(8,128)(2,1)S(1)}, u32[]{:S(2)}, u32[]{:S(2)}) collective-permute-start(bf16[128,2560]{1,0:T(8,128)(2,1)} %add_convert_fusion.2), channel_id=1, source_target_pairs={{32,0},{64,32},{96,64},{128,96},{160,128},{192,160},{224,192},{33,... | collective-permute-start | bytes 1966088 | tf_op jit(solution)/shard_map/while/body/eval_jaxpr/ppermute | solution.py:13
  87.1 17.6 %collective-permute-start = (bf16[128,2560]{1,0:T(8,128)(2,1)}, bf16[128,2560]{1,0:T(8,128)(2,1)S(1)}, u32[]{:S(2)}, u32[]{:S(2)}) collective-permute-start(bf16[128,2560]{1,0:T(8,128)(2,1)} %add_convert_fusion.2), channel_id=1, source_target_pairs={{32,0},{64,32},{96,64},{128,96},{160,128},{192,160},{224,192},{33,... | collective-permute-start | bytes 1966088 | tf_op jit(solution)/shard_map/while/body/eval_jaxpr/ppermute | solution.py:13
  110.6 15.4 %collective-permute-start = (bf16[128,2560]{1,0:T(8,128)(2,1)}, bf16[128,2560]{1,0:T(8,128)(2,1)S(1)}, u32[]{:S(2)}, u32[]{:S(2)}) collective-permute-start(bf16[128,2560]{1,0:T(8,128)(2,1)} %add_convert_fusion.2), channel_id=1, source_target_pairs={{32,0},{64,32},{96,64},{128,96},{160,128},{192,160},{224,192},{33,... | collective-permute-start | bytes 1966088 | tf_op jit(solution)/shard_map/while/body/eval_jaxpr/ppermute | solution.py:13
  131.9 14.5 %collective-permute-start = (bf16[128,2560]{1,0:T(8,128)(2,1)}, bf16[128,2560]{1,0:T(8,128)(2,1)S(1)}, u32[]{:S(2)}, u32[]{:S(2)}) collective-permute-start(bf16[128,2560]{1,0:T(8,128)(2,1)} %add_convert_fusion.2), channel_id=1, source_target_pairs={{32,0},{64,32},{96,64},{128,96},{160,128},{192,160},{224,192},{33,... | collective-permute-start | bytes 1966088 | tf_op jit(solution)/shard_map/while/body/eval_jaxpr/ppermute | solution.py:13
  152.3 13.6 %collective-permute-start = (bf16[128,2560]{1,0:T(8,128)(2,1)}, bf16[128,2560]{1,0:T(8,128)(2,1)S(1)}, u32[]{:S(2)}, u32[]{:S(2)}) collective-permute-start(bf16[128,2560]{1,0:T(8,128)(2,1)} %add_convert_fusion.2), channel_id=1, source_target_pairs={{32,0},{64,32},{96,64},{128,96},{160,128},{192,160},{224,192},{33,... | collective-permute-start | bytes 1966088 | tf_op jit(solution)/shard_map/while/body/eval_jaxpr/ppermute | solution.py:13
  166.1 6.9 %copy-start.4 = (f32[1,512,8]{1,2,0:T(8,128)S(1)}, f32[1,512,8]{1,2,0:T(8,128)}, u32[]{:S(2)}) copy-start(f32[1,512,8]{1,2,0:T(8,128)} %param.21) | copy-start | bytes 49156
  172.9 8.0 %copy-start.1 = (bf16[2560,512]{1,0:T(8,128)(2,1)S(1)}, bf16[2560,512]{1,0:T(8,128)(2,1)}, u32[]{:S(2)}) copy-start(bf16[2560,512]{1,0:T(8,128)(2,1)} %get-tuple-element.340) | copy-start | bytes 7864324
  180.6 365.2 %all-reduce.6.cloned.1.call-start = ((), (), s32[]{:S(2)}) async-start(), calls=%async_computation.1 | async-start | bytes 163840 | tf_op jit(solution)/shard_map/psum | solution.py:104
Sparse Core Ops, SparseCore 0:
  180.8 115.4 all-reduce.3
  437.0 108.8 all-reduce.5
where the time goes:
time: 555 us; the launch traced here: 554 us
  waiting for transfers between devices  317 us (57%)
  blocking collectives  121 us (22%)
  matrix products  72.2 us (13%)
  other arithmetic  18.1 us (3%)
  between operations  14.9 us (3%)
  starting transfers between devices  9.22 us (2%)
    psum x1, blocking collectives, shards(): lax.psum((contract_rows(m_value, basis_value), contract_rows(m_out, basis...  121 us
    psum x1, waiting for transfers between devices, shards(): lax.psum((contract_rows(m_value, basis_value), contract_rows(m_out, basis...  109 us
    ppermute x7, waiting for transfers between devices, shifted(): return lax.ppermute(block, axis, route)  105 us
    psum x1, waiting for transfers between devices, shards(): total_value, total_out = lax.psum((p_value, p_out), 'dp')  103 us
    dot_general x7, matrix products, branch_back(): lax.dot_general(value_grad, w_val, (((1,), (1,)), ((), ())), preferred_el...  31.2 us
    dot_general x4, matrix products, contract_rows(): lax.dot_general(left_side, right_side, (((0,), (0,)), ((), ())), precisio...  12.5 us
  transfers between devices with their start and end apart: 9, of which 9 were waited for; matrix products, arithmetic and copies ran while one was open for 2% of the time, Pallas kernels for 0%

commit v1 on v0

v1 whole, which is shorter than its diff:
```python
import functools

import jax
import jax.numpy as jnp
from jax import lax
from jax.experimental import pallas as pl
from jax.experimental.pallas import tpu as pltpu
from jax.sharding import PartitionSpec as P

EPSILON = 1e-06
LANES = 128
BF16 = jnp.bfloat16
F32 = jnp.float32


def mm(a, b):
    return lax.dot_general(a, b, (((1,), (0,)), ((), ())), preferred_element_type=F32)


def mm_nt(a, b):
    return lax.dot_general(a, b, (((1,), (1,)), ((), ())), preferred_element_type=F32)


def split(x):
    high = x.astype(BF16).astype(F32)
    return jnp.concatenate([high, x - high], axis=0).astype(BF16)


def joined(product):
    half = product.shape[0] // 2
    return product[:half] + product[half:]


def small_mm(x, big):
    return joined(mm(split(x), big))


def small_mm_nt(x, big):
    return joined(mm_nt(split(x), big))


def inverse_factor(gram):
    n = gram.shape[0]
    row = lax.broadcasted_iota(jnp.int32, (n, n), 0)
    col = lax.broadcasted_iota(jnp.int32, (n, n), 1)
    work = jnp.concatenate([gram, jnp.where(row == col, 1.0, 0.0)], axis=1)
    line = lax.broadcasted_iota(jnp.int32, (n, 2 * n), 0)
    for k in range(n):
        root = lax.rsqrt(work[k : k + 1, k : k + 1])
        pivot = work[k : k + 1, :] * root
        factor = work[:, k : k + 1] * root
        work = jnp.where(line == k, pivot, jnp.where(line > k, work - factor * pivot, work))
    return work[:, n:]


def apply_small(lower, tile):
    total = lower[:, 0:1] * tile[0:1, :]
    for k in range(1, lower.shape[1]):
        total = total + lower[:, k : k + 1] * tile[k : k + 1, :]
    return total


def kernel(
    sections,
    replicas,
    blocks,
    acts_hbm,
    top_hbm,
    count_ref,
    gain_hbm,
    w_value_hbm,
    w_out_hbm,
    err_value_hbm,
    err_out_hbm,
    q_value_hbm,
    q_out_hbm,
    out_value,
    out_out,
    acts,
    top,
    gain,
    w_value,
    w_out,
    err_value,
    err_out,
    start_value,
    start_out,
    w_value_t,
    w_out_t,
    unit,
    inv_rms,
    normed,
    values,
    grads,
    passed,
    value_grad,
    norm_grad,
    p_part,
    p_all,
    q_part,
    q_all,
    p_seen,
    q_seen,
    load_sem,
    relay_send,
    relay_recv,
    reduce_send,
    reduce_recv,
):
    section = lax.axis_index("section")
    me = lax.axis_index("dp")
    rows, dw = acts.shape
    hv = w_out.shape[0]
    size = rows // blocks
    value_tiles, out_tiles = dw // LANES, hv // LANES
    tiles = value_tiles + out_tiles
    last = sections - 1

    loads = [
        pltpu.make_async_copy(src, dst, load_sem.at[i])
        for i, (src, dst) in enumerate(
            [
                (w_out_hbm, w_out),
                (top_hbm, top),
                (acts_hbm, acts),
                (gain_hbm, gain),
                (w_value_hbm, w_value),
                (q_value_hbm, start_value),
                (q_out_hbm, start_out),
                (err_value_hbm, err_value),
                (err_out_hbm, err_out),
            ]
        )
    ]
    for load in loads:
        load.start()
    (l_w_out, l_top, l_acts, l_gain, l_w_value, l_q_value, l_q_out, l_err_value, l_err_out) = loads

    barrier = pltpu.get_barrier_semaphore()

    def greet(k, carry):
        pl.semaphore_signal(
            barrier, inc=1, device_id={"dp": lax.rem(me + k, replicas)}, device_id_type=pl.DeviceIdType.MESH
        )
        return carry

    for step in (1, sections - 1):
        pl.semaphore_signal(
            barrier,
            inc=1,
            device_id={"section": lax.rem(section + step, sections)},
            device_id_type=pl.DeviceIdType.MESH,
        )
    lax.fori_loop(1, replicas, greet, 0)

    count = count_ref[0]
    scale = 1.0 / jnp.full((1, 1), count, jnp.int32).astype(F32)

    def block_rows(b):
        return pl.ds(pl.multiple_of(b * size, size), size)

    def normalise():
        def body(b, carry):
            here = block_rows(b)
            wide = acts[here, :].astype(F32)
            inv = lax.rsqrt(jnp.mean(wide * wide, axis=-1, keepdims=True) + EPSILON)
            unit_rows = wide * inv
            inv_rms[here, :] = jnp.broadcast_to(inv, (size, LANES))
            unit[here, :] = unit_rows
            normed[here, :] = (unit_rows * gain[...]).astype(BF16)
            return carry

        lax.fori_loop(0, blocks, body, 0)

    def error_parts():
        p_part[:, :dw] = small_mm_nt(start_value[...], err_value[...])
        p_part[:, dw:] = small_mm_nt(start_out[...], err_out[...])

    def hop(b):
        here = block_rows(b)
        return pltpu.make_async_remote_copy(
            src_ref=passed.at[here],
            dst_ref=grads.at[here],
            send_sem=relay_send.at[b],
            recv_sem=relay_recv.at[b],
            device_id={"section": lax.rem(section + last, sections)},
            device_id_type=pl.DeviceIdType.MESH,
        )

    def pass_on(b, product):
        here = block_rows(b)
        scaled = product * gain[...]
        unit_rows = unit[here, :]
        centred = scaled - unit_rows * jnp.mean(scaled * unit_rows, axis=-1, keepdims=True)
        inv = inv_rms[here, 0:1]
        passed[here, :] = (grads[here, :].astype(F32) + inv * centred).astype(BF16)
        hop(b).start()

    @pl.when(section == last)
    def _():
        l_top.wait()
        live = lax.broadcasted_iota(jnp.int32, (rows, 1), 0) < count
        grads[...] = jnp.where(live, top[...].astype(F32), 0.0).astype(BF16)
        l_w_out.wait()
        value_grad[...] = mm_nt(grads[...], w_out[...]).astype(BF16)
        l_acts.wait()
        l_gain.wait()
        normalise()
        l_w_value.wait()
        norm_grad[...] = mm_nt(value_grad[...], w_value[...])
        pl.semaphore_wait(barrier, replicas + 1)

        def body(b, carry):
            pass_on(b, norm_grad[block_rows(b), :])
            return carry

        lax.fori_loop(0, blocks, body, 0)
        values[...] = mm(normed[...], w_value[...]).astype(BF16)
        for load in (l_q_value, l_q_out, l_err_value, l_err_out):
            load.wait()
        error_parts()

    @pl.when(section < last)
    def _():
        l_w_out.wait()
        w_out_t[...] = w_out[...].T
        l_acts.wait()
        l_gain.wait()
        normalise()
        l_w_value.wait()
        w_value_t[...] = w_value[...].T
        values[...] = mm(normed[...], w_value[...]).astype(BF16)
        for load in (l_top, l_q_value, l_q_out, l_err_value, l_err_out):
            load.wait()
        error_parts()
        pl.semaphore_wait(barrier, replicas + 1)

        def body(b, carry):
            here = block_rows(b)
            hop(b).wait_recv()
            v_rows = mm(grads[here, :], w_out_t[...]).astype(BF16)
            value_grad[here, :] = v_rows

            @pl.when(section > 0)
            def _():
                pass_on(b, mm(v_rows, w_value_t[...]))

            return carry

        lax.fori_loop(0, blocks, body, 0)

    def exchange(part, seen, total, phase, finish):
        def tile(ref, j):
            return ref.at[:, pl.ds(pl.multiple_of(j * LANES, LANES), LANES)]

        def scatter(k, carry):
            owner = lax.rem(me + k, replicas)

            @pl.when(owner < tiles)
            def _():
                pltpu.make_async_remote_copy(
                    src_ref=tile(part, owner),
                    dst_ref=seen.at[me],
                    send_sem=reduce_send.at[2 * phase],
                    recv_sem=reduce_recv.at[2 * phase],
                    device_id={"dp": owner},
                    device_id_type=pl.DeviceIdType.MESH,
                ).start()

            return carry

        lax.fori_loop(1, replicas, scatter, 0)
        extra = finish[0]()

        def arrivals(sem, amount):
            return pltpu.make_async_copy(seen.at[pl.ds(0, amount)], seen.at[pl.ds(0, amount)], sem)

        def spread(k):
            return pltpu.make_async_remote_copy(
                src_ref=tile(total, me),
                dst_ref=tile(total, me),
                send_sem=reduce_send.at[2 * phase + 1],
                recv_sem=reduce_recv.at[2 * phase + 1],
                device_id={"dp": lax.rem(me + k, replicas)},
                device_id_type=pl.DeviceIdType.MESH,
            )

        @pl.when(me < tiles)
        def _():
            seen[me] = tile(part, me)[...]
            arrivals(reduce_recv.at[2 * phase], replicas - 1).wait()
            tile(total, me)[...] = finish[1](jnp.sum(seen[...], axis=0), extra)

            def body(k, carry):
                spread(k).start()
                return carry

            lax.fori_loop(1, replicas, body, 0)
            arrivals(reduce_recv.at[2 * phase + 1], tiles - 1).wait()
            arrivals(reduce_send.at[2 * phase], tiles - 1).wait()
            arrivals(reduce_send.at[2 * phase + 1], replicas - 1).wait()

        @pl.when(me >= tiles)
        def _():
            arrivals(reduce_recv.at[2 * phase + 1], tiles).wait()
            arrivals(reduce_send.at[2 * phase], tiles).wait()

    p_part[:, :dw] += small_mm(small_mm_nt(start_value[...], value_grad[...]) * scale, normed[...])
    p_part[:, dw:] += small_mm(small_mm_nt(start_out[...], grads[...]) * scale, values[...])
    exchange(p_part, p_seen, p_all, 0, (lambda: None, lambda tile, extra: tile))

    p_value, p_out = p_all[:, :dw], p_all[:, dw:]
    q_part[:, :hv] = small_mm(small_mm_nt(p_value, normed[...]) * scale, value_grad[...]) + small_mm(
        p_value, err_value[...]
    )
    q_part[:, hv:] = small_mm(small_mm_nt(p_out, values[...]) * scale, grads[...]) + small_mm(
        p_out, err_out[...]
    )

    def factors():
        grams = [
            lax.dot_general(
                x, x, (((1,), (1,)), ((), ())), precision=lax.Precision.HIGHEST, preferred_element_type=F32
            )
            for x in (p_all[:, :dw], p_all[:, dw:])
        ]
        return [inverse_factor(gram) for gram in grams]

    def solved(tile, extra):
        for_value, for_out = extra
        return apply_small(jnp.where(me < out_tiles, for_value, for_out), tile)

    exchange(q_part, q_seen, q_all, 1, (factors, solved))
    out_value[...] = q_all[:, :hv]
    out_out[...] = q_all[:, hv:]

    @pl.when(section > 0)
    def _():
        def body(b, carry):
            hop(b).wait_send()
            return carry

        lax.fori_loop(0, blocks, body, 0)


def solution(mesh):
    sections, replicas = mesh.shape["section"], mesh.shape["dp"]

    def shards(
        acts, out_grad, tok_count, norm_gain, w_value, w_out, err_value, err_out, start_q_value, start_q_out
    ):
        rows, dw = out_grad.shape
        hv, rank = start_q_value.shape[1:]
        blocks = rows // 16
        any_space = pl.BlockSpec(memory_space=pl.ANY)
        vmem = pl.BlockSpec(memory_space=pltpu.VMEM)
        q_value, q_out = pl.pallas_call(
            functools.partial(kernel, sections, replicas, blocks),
            out_shape=(
                jax.ShapeDtypeStruct((rank, hv), F32),
                jax.ShapeDtypeStruct((rank, dw), F32),
            ),
            in_specs=[any_space] * 2 + [pl.BlockSpec(memory_space=pltpu.SMEM)] + [any_space] * 7,
            out_specs=(vmem, vmem),
            scratch_shapes=[
                pltpu.VMEM((rows, dw), BF16),
                pltpu.VMEM((rows, dw), BF16),
                pltpu.VMEM((1, dw), F32),
                pltpu.VMEM((dw, hv), BF16),
                pltpu.VMEM((hv, dw), BF16),
                pltpu.VMEM((dw, hv), BF16),
                pltpu.VMEM((hv, dw), BF16),
                pltpu.VMEM((rank, hv), F32),
                pltpu.VMEM((rank, dw), F32),
                pltpu.VMEM((hv, dw), BF16),
                pltpu.VMEM((dw, hv), BF16),
                pltpu.VMEM((rows, dw), F32),
                pltpu.VMEM((rows, LANES), F32),
                pltpu.VMEM((rows, dw), BF16),
                pltpu.VMEM((rows, hv), BF16),
                pltpu.VMEM((rows, dw), BF16),
                pltpu.VMEM((rows, dw), BF16),
                pltpu.VMEM((rows, hv), BF16),
                pltpu.VMEM((rows, dw), F32),
                pltpu.VMEM((rank, dw + hv), F32),
                pltpu.VMEM((rank, dw + hv), F32),
                pltpu.VMEM((rank, dw + hv), F32),
                pltpu.VMEM((rank, dw + hv), F32),
                pltpu.VMEM((replicas, rank, LANES), F32),
                pltpu.VMEM((replicas, rank, LANES), F32),
                pltpu.SemaphoreType.DMA((9,)),
                pltpu.SemaphoreType.DMA((blocks,)),
                pltpu.SemaphoreType.DMA((blocks,)),
                pltpu.SemaphoreType.DMA((4,)),
                pltpu.SemaphoreType.DMA((4,)),
            ],
            compiler_params=pltpu.CompilerParams(
                collective_id=0, has_side_effects=True, vmem_limit_bytes=48 * 2**20
            ),
            cost_estimate=pl.CostEstimate(flops=1_700_000_000, bytes_accessed=12_000_000, transcendentals=0),
        )(
            acts[0],
            out_grad,
            tok_count,
            norm_gain,
            w_value[0],
            w_out[0],
            err_value[0],
            err_out[0],
            start_q_value[0].T,
            start_q_out[0].T,
        )
        return q_value.T[None], q_out.T[None]

    placed = (
        P("section", "dp", None),
        P("dp", None),
        P("dp"),
        P("section", None),
        P("section", None, None),
        P("section", None, None),
        P("section", "dp", None),
        P("section", "dp", None),
        P("section", None, None),
        P("section", None, None),
    )
    return jax.shard_map(
        shards,
        mesh=mesh,
        in_specs=placed,
        out_specs=(P("section", None, None), P("section", None, None)),
        check_vma=False,
    )
```

time: 555 us -> 88.9 us (0.16)
  waiting for transfers between devices: 317 us -> 0 us
  blocking collectives: 121 us -> 0 us
  Pallas kernels: 0 us -> 79.8 us
  matrix products: 72.2 us -> 0 us
  other arithmetic: 18.1 us -> 0 us
  between operations: 14.9 us -> 1.3 us
  starting transfers between devices: 9.22 us -> 0 us
  local copies, waits for them, and re-layouts: 1.7 us -> 7.45 us
    psum x2 -> x0, waiting for transfers between devices: 212 us -> none  [the longest x1 109 us: shards(): lax.psum((contract_rows(m_value, basis_value), contract_rows(m_out, basis...]
    psum x1 -> x0, blocking collectives: 121 us -> none  [shards(): lax.psum((contract_rows(m_value, basis_value), contract_rows(m_out, basis...]
    ppermute x7 -> x0, waiting for transfers between devices: 105 us -> none  [shifted(): return lax.ppermute(block, axis, route)]
    pallas_call x0 -> x1, Pallas kernels: none -> 79.8 us  [shards(): pl.pallas_call(functools.partial(kernel, sections, replicas, blocks), out...]
    dot_general x15 -> x0, matrix products: 70.8 us -> none  [the longest x7 31.2 us: branch_back(): lax.dot_general(value_grad, w_val, (((1,), (1,)), ((), ())), preferred_el...]
    ppermute x7 -> x0, starting transfers between devices: 8.96 us -> none  [shifted(): return lax.ppermute(block, axis, route)]
    convert_element_type x7 -> x0, other arithmetic: 8.49 us -> none  [branch_back(): (incoming.astype(jnp.float32) + inv_rms * centred).astype(jnp.bfloat16)]
    unnamed x11 -> x14, local copies, waits for them, and re-layouts: 1.55 us -> 7.45 us
  transfers between devices with their start and end apart: 9 -> 0, of which waited for: 9 -> 0; matrix products, arithmetic and copies ran while one was open for 2% -> 0% of each run, Pallas kernels for 0% -> 0%
where the time goes in v1:
time: 88.9 us; the launch traced here: 88.5 us
  Pallas kernels  79.8 us (90%)
  local copies, waits for them, and re-layouts  7.45 us (8%)
  between operations  1.3 us (1%)
    pallas_call x1, Pallas kernels, shards(): pl.pallas_call(functools.partial(kernel, sections, replicas, blocks), out...  79.8 us
    unnamed x14, local copies, waits for them, and re-layouts  7.45 us

profile of v1, /device:TPU:1, one launch (start us, length us, event | category | flops | bytes accessed | tf_op | source)
XLA Modules:
  0.0 88.5 jit_solution(11996395743816490629)
XLA Ops:
  1.3 0.0 copy-start
  1.3 1.7 %copy-done = bf16[1,2560,512]{2,1,0:T(8,128)(2,1)S(1)} copy-done((bf16[1,2560,512]{2,1,0:T(8,128)(2,1)S(1)}, bf16[1,2560,512]{2,1,0:T(8,128)(2,1)}, u32[]{:S(2)}) %copy-start) | copy-done | bytes 2621464
  3.0 0.0 copy-start.1
  3.0 1.1 %copy-done.1 = bf16[1,128,2560]{2,1,0:T(8,128)(2,1)S(1)} copy-done((bf16[1,128,2560]{2,1,0:T(8,128)(2,1)S(1)}, bf16[1,128,2560]{2,1,0:T(8,128)(2,1)}, u32[]{:S(2)}) %copy-start.1) | copy-done | bytes 655384
  4.1 0.0 copy-start.2
  4.1 1.1 %copy-done.2 = bf16[128,2560]{1,0:T(8,128)(2,1)S(1)} copy-done((bf16[128,2560]{1,0:T(8,128)(2,1)S(1)}, bf16[128,2560]{1,0:T(8,128)(2,1)}, u32[]{:S(2)}) %copy-start.2) | copy-done | bytes 655384
  5.2 0.0 copy-start.3
  5.2 0.9 copy-done.3
  6.1 0.0 copy-start.4
  6.1 0.7 copy-done.4
  6.8 0.0 copy-start.5
  6.8 0.7 copy-done.5
  7.5 79.8 %shard_map.113 = (f32[8,512]{1,0:T(8,128)S(1)}, f32[8,2560]{1,0:T(8,128)S(1)}) custom-call(bf16[128,2560]{1,0:T(8,128)(2,1)S(1)} %bitcast.18, bf16[128,2560]{1,0:T(8,128)(2,1)S(1)} %copy-done.2, s32[1]{0:T(128)S(6)} %copy.14.count_ref, f32[1,2560]{1,0:T(1,128)S(1)} %copy-done.5, bf16[2560,512]{1,0:T(8,128)(2,1)S(1)} %bitcast.17, bf16[512,2560]{1,0:T(8,128)(2,1)} %bitcast.23, ...), custom_call_target="tpu_custom_call" | custom-call | flops 1700000000 | bytes 12000000 | tf_op jit(solution)/shard_map/pallas_call | solution.py:357
  87.3 0.6 copy.15
  87.9 0.6 copy.16
Async XLA Ops:
  1.3 1.7 %copy-start = (bf16[1,2560,512]{2,1,0:T(8,128)(2,1)S(1)}, bf16[1,2560,512]{2,1,0:T(8,128)(2,1)}, u32[]{:S(2)}) copy-start(bf16[1,2560,512]{2,1,0:T(8,128)(2,1)} %param.14) | copy-start | bytes 7864324
  3.0 1.1 %copy-start.1 = (bf16[1,128,2560]{2,1,0:T(8,128)(2,1)S(1)}, bf16[1,128,2560]{2,1,0:T(8,128)(2,1)}, u32[]{:S(2)}) copy-start(bf16[1,128,2560]{2,1,0:T(8,128)(2,1)} %param.10) | copy-start | bytes 1966084
  4.1 1.1 %copy-start.2 = (bf16[128,2560]{1,0:T(8,128)(2,1)S(1)}, bf16[128,2560]{1,0:T(8,128)(2,1)}, u32[]{:S(2)}) copy-start(bf16[128,2560]{1,0:T(8,128)(2,1)} %top_hbm.1) | copy-start | bytes 1966084
  5.2 0.9 %copy-start.3 = (f32[1,2560,8]{1,2,0:T(8,128)S(1)}, f32[1,2560,8]{1,2,0:T(8,128)}, u32[]{:S(2)}) copy-start(f32[1,2560,8]{1,2,0:T(8,128)} %param.19) | copy-start | bytes 245764
  6.1 0.7 copy-start.4
  6.8 0.7 copy-start.5

commit v2 on v1

v2 whole, which is shorter than its diff:
```python
import functools

import jax
import jax.numpy as jnp
from jax import lax
from jax.experimental import pallas as pl
from jax.experimental.pallas import tpu as pltpu
from jax.sharding import PartitionSpec as P

EPSILON = 1e-06
LANES = 128
CUTS = (0, 5, 10, 15, 20)
GROUPS = ((0,), (1,), (2,), (3,))
BF16 = jnp.bfloat16
F32 = jnp.float32


def mm(a, b):
    return lax.dot_general(a, b, (((1,), (0,)), ((), ())), preferred_element_type=F32)


def mm_nt(a, b):
    return lax.dot_general(a, b, (((1,), (1,)), ((), ())), preferred_element_type=F32)


def split(x):
    high = x.astype(BF16).astype(F32)
    return jnp.concatenate([high, x - high], axis=0).astype(BF16)


def joined(product):
    half = product.shape[0] // 2
    return product[:half] + product[half:]


def small_mm(x, big):
    return joined(mm(split(x), big))


def small_mm_nt(x, big):
    return joined(mm_nt(split(x), big))


def inverse_factor(gram):
    n = gram.shape[0]
    row = lax.broadcasted_iota(jnp.int32, (n, n), 0)
    col = lax.broadcasted_iota(jnp.int32, (n, n), 1)
    work = jnp.concatenate([gram, jnp.where(row == col, 1.0, 0.0)], axis=1)
    line = lax.broadcasted_iota(jnp.int32, (n, 2 * n), 0)
    for k in range(n):
        root = lax.rsqrt(work[k : k + 1, k : k + 1])
        pivot = work[k : k + 1, :] * root
        factor = work[:, k : k + 1] * root
        work = jnp.where(line == k, pivot, jnp.where(line > k, work - factor * pivot, work))
    return work[:, n:]


def apply_small(lower, tile):
    total = lower[:, 0:1] * tile[0:1, :]
    for k in range(1, lower.shape[1]):
        total = total + lower[:, k : k + 1] * tile[k : k + 1, :]
    return total


def kernel(
    sections,
    replicas,
    blocks,
    cuts,
    groups,
    acts_hbm,
    top_hbm,
    count_ref,
    gain_hbm,
    w_value_hbm,
    w_out_hbm,
    err_value_hbm,
    err_out_hbm,
    q_value_hbm,
    q_out_hbm,
    out_ref,
    acts,
    top,
    gain,
    w_value,
    w_out,
    err_value,
    err_out,
    start_value,
    start_out,
    w_value_t,
    w_out_t,
    unit,
    inv_rms,
    normed,
    values,
    values_wide,
    grads,
    passed,
    value_grad,
    norm_grad,
    p_part,
    p_all,
    p_packed,
    q_packed,
    p_total,
    q_total,
    p_seen,
    q_seen,
    load_sem,
    relay_send,
    relay_recv,
    reduce_send,
    reduce_recv,
):
    section = lax.axis_index("section")
    me = lax.axis_index("dp")
    rows, dw = acts.shape
    hv = w_out.shape[0]
    size = rows // blocks
    value_tiles, out_tiles = dw // (2 * LANES), hv // (2 * LANES)
    tiles = value_tiles + out_tiles
    last = sections - 1
    chips = replicas // 2
    chip, core = me // 2, lax.rem(me, 2)
    owner = (core == 1) & (chip < tiles)
    pieces = len(cuts) - 1

    loads = [
        pltpu.make_async_copy(src, dst, load_sem.at[i])
        for i, (src, dst) in enumerate(
            [
                (top_hbm, top),
                (w_out_hbm, w_out),
                (acts_hbm, acts),
                (gain_hbm, gain),
                (w_value_hbm, w_value),
                (q_value_hbm, start_value),
                (q_out_hbm, start_out),
                (err_value_hbm, err_value),
                (err_out_hbm, err_out),
            ]
        )
    ]
    (l_top, l_w_out, l_acts, l_gain, l_w_value, l_q_value, l_q_out, l_err_value, l_err_out) = loads
    for load in loads[:4]:
        load.start()

    barrier = pltpu.get_barrier_semaphore()

    def greet(k, carry):
        pl.semaphore_signal(
            barrier, inc=1, device_id={"dp": lax.rem(me + k, replicas)}, device_id_type=pl.DeviceIdType.MESH
        )
        return carry

    for step in (1, sections - 1):
        pl.semaphore_signal(
            barrier,
            inc=1,
            device_id={"section": lax.rem(section + step, sections)},
            device_id_type=pl.DeviceIdType.MESH,
        )
    lax.fori_loop(1, replicas, greet, 0)

    count = count_ref[0]
    scale = 1.0 / jnp.full((1, 1), count, jnp.int32).astype(F32)

    def block_rows(b):
        return pl.ds(pl.multiple_of(b * size, size), size)

    def normalise(b):
        here = block_rows(b)
        wide = acts[here, :].astype(F32)
        inv = lax.rsqrt(jnp.mean(wide * wide, axis=-1, keepdims=True) + EPSILON)
        unit_rows = wide * inv
        inv_rms[here, :] = jnp.broadcast_to(inv, (size, LANES))
        unit[here, :] = unit_rows
        normed[here, :] = (unit_rows * gain[...]).astype(BF16)

    def each_block(work):
        def body(b, carry):
            work(b)
            return carry

        lax.fori_loop(0, blocks, body, 0)

    def error_parts():
        p_part[:, :dw] = small_mm_nt(start_value[...], err_value[...])
        p_part[:, dw:] = small_mm_nt(start_out[...], err_out[...])

    def add_block(here):
        p_part[:, :dw] += small_mm(small_mm_nt(start_value[...], value_grad[here, :]) * scale, normed[here, :])
        p_part[:, dw:] += small_mm(small_mm_nt(start_out[...], grads[here, :]) * scale, values[here, :])

    def piece(c):
        return slice(cuts[c], cuts[c + 1])

    def hop(b, c):
        return pltpu.make_async_remote_copy(
            src_ref=passed.at[block_rows(b), piece(c)],
            dst_ref=grads.at[block_rows(b), piece(c)],
            send_sem=relay_send.at[b * pieces + c],
            recv_sem=relay_recv.at[b * pieces + c],
            device_id={"section": lax.rem(section + last, sections)},
            device_id_type=pl.DeviceIdType.MESH,
        )

    def pass_on(b, mean, product):
        here = block_rows(b)
        inv = inv_rms[here, 0:1]
        for c in range(pieces):
            cols = piece(c)
            centred = product(cols) * gain[:, cols] - unit[here, cols] * mean
            passed[here, cols] = (grads[here, cols].astype(F32) + inv * centred).astype(BF16)
            if c + 1 == 2:
                for early in range(2):
                    hop(b, early).start()
        for c in range(2, pieces):
            hop(b, c).start()

    def project():
        wide = mm(normed[...], w_value[...])
        values_wide[...] = wide
        values[...] = wide.astype(BF16)

    @pl.when(section == last)
    def _():
        l_top.wait()
        l_w_value.start()
        live = lax.broadcasted_iota(jnp.int32, (rows, 1), 0) < count
        grads[...] = jnp.where(live, top[...].astype(F32), 0.0).astype(BF16)
        l_w_out.wait()
        value_grad[...] = mm_nt(grads[...], w_out[...]).astype(BF16)
        l_acts.wait()
        l_gain.wait()
        l_w_value.wait()
        for load in loads[5:]:
            load.start()
        norm_grad[...] = mm_nt(value_grad[...], w_value[...])
        pl.semaphore_wait(barrier, replicas + 1)

        def send(b):
            here = block_rows(b)
            normalise(b)
            mean = jnp.mean(norm_grad[here, :] * gain[...] * unit[here, :], axis=-1, keepdims=True)
            pass_on(b, mean, lambda cols: norm_grad[here, cols])

        each_block(send)
        project()
        for load in loads[5:]:
            load.wait()
        error_parts()

    @pl.when(section < last)
    def _():
        l_acts.wait()
        l_w_value.start()
        l_gain.wait()
        for load in loads[5:]:
            load.start()
        each_block(normalise)
        l_w_out.wait()
        w_out_t[...] = w_out[...].T
        l_w_value.wait()
        w_value_t[...] = w_value[...].T
        project()
        for load in (l_top, *loads[5:]):
            load.wait()
        error_parts()
        pl.semaphore_wait(barrier, replicas + 1)

        def relay(b):
            here = block_rows(b)
            total = None
            for group in groups:
                for c in group:
                    hop(b, c).wait_recv()
                cols = slice(cuts[group[0]], cuts[group[-1] + 1])
                term = mm(grads[here, cols], w_out_t[cols, :])
                total = term if total is None else total + term
            v_rows = total.astype(BF16)
            value_grad[here, :] = v_rows

            @pl.when(section > 0)
            def _():
                mean = jnp.sum(v_rows.astype(F32) * values_wide[here, :], axis=-1, keepdims=True) * (1.0 / dw)
                pass_on(b, mean, lambda cols: mm(v_rows, w_value_t[:, cols]))

            @pl.when(section == 0)
            def _():
                add_block(here)

        each_block(relay)

    def packed(x):
        return jnp.concatenate([x[:, :LANES], x[:, LANES:]], axis=0).astype(BF16)

    def arrivals(ref, amount, sem):
        return pltpu.make_async_copy(ref.at[pl.ds(0, amount)], ref.at[pl.ds(0, amount)], sem)

    def far_first(k):
        return lax.rem(chip + chips // 2 + 2 + k, chips)

    def exchange(part, seen, total, phase, meanwhile, finish):
        def scatter(k, carry):
            to = far_first(k)

            @pl.when((to < tiles) & ((to != chip) | (core == 0)))
            def _():
                pltpu.make_async_remote_copy(
                    src_ref=part.at[to],
                    dst_ref=seen.at[me],
                    send_sem=reduce_send.at[2 * phase],
                    recv_sem=reduce_recv.at[2 * phase],
                    device_id={"dp": 2 * to + 1},
                    device_id_type=pl.DeviceIdType.MESH,
                ).start()

            return carry

        lax.fori_loop(0, chips, scatter, 0)
        extra = meanwhile()

        @pl.when(owner)
        def _():
            seen[me] = part[chip]
            arrivals(seen, replicas - 1, reduce_recv.at[2 * phase]).wait()
            total[chip] = finish(jnp.sum(seen[...].astype(F32), axis=0), extra).astype(BF16)

            def spread(k, carry):
                to = far_first(k)
                for end in range(2):

                    @pl.when((to != chip) | (end == 0))
                    def _():
                        pltpu.make_async_remote_copy(
                            src_ref=total.at[chip],
                            dst_ref=total.at[chip],
                            send_sem=reduce_send.at[2 * phase + 1],
                            recv_sem=reduce_recv.at[2 * phase + 1],
                            device_id={"dp": 2 * to + end},
                            device_id_type=pl.DeviceIdType.MESH,
                        ).start()

                return carry

            lax.fori_loop(0, chips, spread, 0)
            arrivals(total, tiles - 1, reduce_recv.at[2 * phase + 1]).wait()

        @pl.when(jnp.logical_not(owner))
        def _():
            arrivals(total, tiles, reduce_recv.at[2 * phase + 1]).wait()

    def finish_sends(seen, phase):
        @pl.when(owner)
        def _():
            arrivals(seen, tiles - 1, reduce_send.at[2 * phase]).wait()
            arrivals(seen, replicas - 1, reduce_send.at[2 * phase + 1]).wait()

        @pl.when(jnp.logical_not(owner))
        def _():
            arrivals(seen, tiles, reduce_send.at[2 * phase]).wait()

    @pl.when(section > 0)
    def _():
        add_block(slice(None))

    for j in range(tiles):
        p_packed[j] = packed(p_part[:, 2 * LANES * j : 2 * LANES * (j + 1)])
    exchange(p_packed, p_seen, p_total, 0, lambda: None, lambda tile, extra: tile)

    def unpacked(first, count):
        halves = [p_total[j] for j in range(first, first + count)]
        return jnp.concatenate([half for tile in halves for half in (tile[:8].astype(F32), tile[8:].astype(F32))], axis=1)

    p_value = unpacked(0, value_tiles)
    p_out = unpacked(value_tiles, out_tiles)
    p_all[:, :dw] = p_value
    p_all[:, dw:] = p_out
    p_value, p_out = p_value.astype(BF16), p_out.astype(BF16)
    q_value = small_mm(mm_nt(p_value, normed[...]) * scale, value_grad[...]) + mm(p_value, err_value[...])
    for j in range(out_tiles):
        q_packed[j] = packed(q_value[:, 2 * LANES * j : 2 * LANES * (j + 1)])
    q_out = small_mm(mm_nt(p_out, values[...]) * scale, grads[...]) + mm(p_out, err_out[...])
    for j in range(value_tiles):
        q_packed[out_tiles + j] = packed(q_out[:, 2 * LANES * j : 2 * LANES * (j + 1)])

    def factors():
        grams = [
            lax.dot_general(
                x, x, (((1,), (1,)), ((), ())), precision=lax.Precision.HIGHEST, preferred_element_type=F32
            )
            for x in (p_all[:, :dw], p_all[:, dw:])
        ]
        return [inverse_factor(gram) for gram in grams]

    def solved(pair, extra):
        for_value, for_out = extra
        lower = jnp.where(chip < out_tiles, for_value, for_out)
        return jnp.concatenate([apply_small(lower, pair[:8]), apply_small(lower, pair[8:])], axis=0)

    exchange(q_packed, q_seen, q_total, 1, factors, solved)
    out_ref[...] = q_total[...]
    finish_sends(p_seen, 0)
    finish_sends(q_seen, 1)

    @pl.when(section > 0)
    def _():
        def sent(b):
            for c in range(pieces):
                hop(b, c).wait_send()

        each_block(sent)


def part_kernel(both, out_value, out_out):
    out_tiles = out_value.shape[1] // (2 * LANES)
    for j in range(both.shape[0]):
        ref, place = (out_value, j) if j < out_tiles else (out_out, j - out_tiles)
        tile = both[j].astype(F32)
        half = tile.shape[0] // 2
        ref[:, 2 * LANES * place : 2 * LANES * place + LANES] = tile[:half]
        ref[:, 2 * LANES * place + LANES : 2 * LANES * (place + 1)] = tile[half:]


def solution(mesh):
    sections, replicas = mesh.shape["section"], mesh.shape["dp"]

    def shards(
        acts, out_grad, tok_count, norm_gain, w_value, w_out, err_value, err_out, start_q_value, start_q_out
    ):
        rows, dw = out_grad.shape
        hv, rank = start_q_value.shape[1:]
        tiles = (dw + hv) // (2 * LANES)
        blocks = rows // 16
        cuts = tuple(cut * dw // CUTS[-1] for cut in CUTS)
        any_space = pl.BlockSpec(memory_space=pl.ANY)
        vmem = pl.BlockSpec(memory_space=pltpu.VMEM)
        both = pl.pallas_call(
            functools.partial(kernel, sections, replicas, blocks, cuts, GROUPS),
            out_shape=pltpu.VMEM((tiles, 2 * rank, LANES), BF16),
            in_specs=[any_space] * 2 + [pl.BlockSpec(memory_space=pltpu.SMEM)] + [any_space] * 7,
            out_specs=vmem,
            scratch_shapes=[
                pltpu.VMEM((rows, dw), BF16),
                pltpu.VMEM((rows, dw), BF16),
                pltpu.VMEM((1, dw), F32),
                pltpu.VMEM((dw, hv), BF16),
                pltpu.VMEM((hv, dw), BF16),
                pltpu.VMEM((dw, hv), BF16),
                pltpu.VMEM((hv, dw), BF16),
                pltpu.VMEM((rank, hv), F32),
                pltpu.VMEM((rank, dw), F32),
                pltpu.VMEM((hv, dw), BF16),
                pltpu.VMEM((dw, hv), BF16),
                pltpu.VMEM((rows, dw), F32),
                pltpu.VMEM((rows, LANES), F32),
                pltpu.VMEM((rows, dw), BF16),
                pltpu.VMEM((rows, hv), BF16),
                pltpu.VMEM((rows, hv), F32),
                pltpu.VMEM((rows, dw), BF16),
                pltpu.VMEM((rows, dw), BF16),
                pltpu.VMEM((rows, hv), BF16),
                pltpu.VMEM((rows, dw), F32),
                pltpu.VMEM((rank, dw + hv), F32),
                pltpu.VMEM((rank, dw + hv), F32),
                pltpu.VMEM((tiles, 2 * rank, LANES), BF16),
                pltpu.VMEM((tiles, 2 * rank, LANES), BF16),
                pltpu.VMEM((tiles, 2 * rank, LANES), BF16),
                pltpu.VMEM((tiles, 2 * rank, LANES), BF16),
                pltpu.VMEM((replicas, 2 * rank, LANES), BF16),
                pltpu.VMEM((replicas, 2 * rank, LANES), BF16),
                pltpu.SemaphoreType.DMA((9,)),
                pltpu.SemaphoreType.DMA((blocks * (len(cuts) - 1),)),
                pltpu.SemaphoreType.DMA((blocks * (len(cuts) - 1),)),
                pltpu.SemaphoreType.DMA((4,)),
                pltpu.SemaphoreType.DMA((4,)),
            ],
            compiler_params=pltpu.CompilerParams(
                collective_id=0, has_side_effects=True, vmem_limit_bytes=60 * 2**20
            ),
            cost_estimate=pl.CostEstimate(flops=1_700_000_000, bytes_accessed=12_000_000, transcendentals=0),
        )(
            acts[0],
            out_grad,
            tok_count,
            norm_gain,
            w_value[0],
            w_out[0],
            err_value[0],
            err_out[0],
            start_q_value[0].T,
            start_q_out[0].T,
        )
        q_value, q_out = pl.pallas_call(
            part_kernel,
            out_shape=(
                jax.ShapeDtypeStruct((rank, hv), F32),
                jax.ShapeDtypeStruct((rank, dw), F32),
            ),
            in_specs=[vmem],
            out_specs=(vmem, vmem),
        )(both)
        return q_value.T[None], q_out.T[None]

    placed = (
        P("section", "dp", None),
        P("dp", None),
        P("dp"),
        P("section", None),
        P("section", None, None),
        P("section", None, None),
        P("section", "dp", None),
        P("section", "dp", None),
        P("section", None, None),
        P("section", None, None),
    )
    return jax.shard_map(
        shards,
        mesh=mesh,
        in_specs=placed,
        out_specs=(P("section", None, None), P("section", None, None)),
        check_vma=False,
    )
```

time: 88.9 us -> 77.2 us (0.87)
  local copies, waits for them, and re-layouts: 7.45 us -> 0.6 us
  Pallas kernels: 79.8 us -> 75.1 us
    unnamed x14 -> x2, local copies, waits for them, and re-layouts: 7.45 us -> 0.6 us
    pallas_call x1 -> x2, Pallas kernels: 79.8 us -> 75.1 us  [the longest x1 73.7 us: shards(): pl.pallas_call(functools.partial(kernel, sections, replicas, blocks, cuts...]
where the time goes in v2:
time: 77.2 us; the launch traced here: 77 us
  Pallas kernels  75.1 us (97%)
  between operations  1.29 us (2%)
    pallas_call x1, Pallas kernels, shards(): pl.pallas_call(functools.partial(kernel, sections, replicas, blocks, cuts...  73.7 us

profile of v2, /device:TPU:1, one launch (start us, length us, event | category | flops | bytes accessed | tf_op | source)
XLA Modules:
  0.0 77.0 jit_solution(10697258058926859830)
XLA Ops:
  1.3 73.7 %shard_map.113.both = bf16[12,16,128]{2,1,0:T(8,128)(2,1)S(1)} custom-call(bf16[128,2560]{1,0:T(8,128)(2,1)} %bitcast.21, bf16[128,2560]{1,0:T(8,128)(2,1)} %top_hbm.1, s32[1]{0:T(128)S(6)} %copy.12.count_ref, f32[1,2560]{1,0:T(1,128)} %gain_hbm.1, bf16[2560,512]{1,0:T(8,128)(2,1)} %bitcast.17, bf16[512,2560]{1,0:T(8,128)(2,1)} %bitcast.18, ...), custom_call_target="tpu_custom_call" | custom-call | flops 1700000000 | bytes 12000000 | tf_op jit(solution)/shard_map/pallas_call | solution.py:440
  75.0 0.0 copy-start
  75.0 0.6 copy-done
  75.6 1.4 %shard_map.114 = (f32[8,512]{1,0:T(8,128)}, f32[8,2560]{1,0:T(8,128)}) custom-call(bf16[12,16,128]{2,1,0:T(8,128)(2,1)} %copy-done), custom_call_target="tpu_custom_call" | custom-call | tf_op jit(solution)/shard_map/pallas_call | solution.py:496
Async XLA Ops:
  75.0 0.6 copy-start

commit v3 on v2

--- a/solution.py
+++ b/solution.py
@@ -11,6 +11,7 @@
 LANES = 128
 CUTS = (0, 5, 10, 15, 20)
 GROUPS = ((0,), (1,), (2,), (3,))
+LIFTED = 2
 BF16 = jnp.bfloat16
 F32 = jnp.float32
 
@@ -112,6 +113,17 @@
     relay_recv,
     reduce_send,
     reduce_recv,
+    lower_normed,
+    lower_values,
+    lower_value_q,
+    lower_out_q,
+    lower_part,
+    lower_packed,
+    lower_seen,
+    lower_total,
+    value_q,
+    lift_send,
+    lift_recv,
 ):
     section = lax.axis_index("section")
     me = lax.axis_index("dp")
@@ -124,6 +136,8 @@
     chips = replicas // 2
     chip, core = me // 2, lax.rem(me, 2)
     owner = (core == 1) & (chip < tiles)
+    lifted = section < LIFTED
+    lifts = (section > 0) & (section <= LIFTED)
     pieces = len(cuts) - 1
 
     loads = [
@@ -163,6 +177,28 @@
         )
     lax.fori_loop(1, replicas, greet, 0)
 
+    @pl.when(lifted)
+    def _():
+        def greet_owner(k, carry):
+            pl.semaphore_signal(
+                barrier,
+                inc=1,
+                device_id={"section": section + 1, "dp": 2 * k + 1},
+                device_id_type=pl.DeviceIdType.MESH,
+            )
+            return carry
+
+        lax.fori_loop(0, tiles, greet_owner, 0)
+
+    def all_here():
+        @pl.when(owner & lifts)
+        def _():
+            pl.semaphore_wait(barrier, 2 * replicas + 1)
+
+        @pl.when(jnp.logical_not(owner & lifts))
+        def _():
+            pl.semaphore_wait(barrier, replicas + 1)
+
     count = count_ref[0]
     scale = 1.0 / jnp.full((1, 1), count, jnp.int32).astype(F32)
 
@@ -192,6 +228,29 @@
     def add_block(here):
         p_part[:, :dw] += small_mm(small_mm_nt(start_value[...], value_grad[here, :]) * scale, normed[here, :])
         p_part[:, dw:] += small_mm(small_mm_nt(start_out[...], grads[here, :]) * scale, values[here, :])
+
+    def add_lower(here):
+        along = small_mm_nt(lower_value_q[...], passed[here, :]) * scale
+        lower_part[:, :dw] += small_mm(along, lower_normed[here, :])
+        along = small_mm_nt(lower_out_q[...], passed[here, :]) * scale
+        lower_part[:, dw:] += small_mm(along, lower_values[here, :])
+
+    def lift(i):
+        src, dst = [
+            (normed, lower_normed),
+            (values, lower_values),
+            (value_q, lower_value_q),
+            (start_out, lower_out_q),
+            (p_part, lower_part),
+        ][i]
+        return pltpu.make_async_remote_copy(
+            src_ref=src,
+            dst_ref=dst,
+            send_sem=lift_send.at[i],
+            recv_sem=lift_recv.at[i],
+            device_id={"section": lax.rem(section + 1, sections)},
+            device_id_type=pl.DeviceIdType.MESH,
+        )
 
     def piece(c):
         return slice(cuts[c], cuts[c + 1])
@@ -238,7 +297,7 @@
         for load in loads[5:]:
             load.start()
         norm_grad[...] = mm_nt(value_grad[...], w_value[...])
-        pl.semaphore_wait(barrier, replicas + 1)
+        all_here()
 
         def send(b):
             here = block_rows(b)
@@ -265,13 +324,30 @@
         l_w_value.wait()
         w_value_t[...] = w_value[...].T
         project()
+        all_here()
+
+
+        @pl.when(lifted)
+        def _():
+            lift(0).start()
+            lift(1).start()
+
         for load in (l_top, *loads[5:]):
             load.wait()
-        error_parts()
-        pl.semaphore_wait(barrier, replicas + 1)
+
+        @pl.when(section < last - 1)
+        def _():
+            error_parts()
+
+        @pl.when(lifted)
+        def _():
+            value_q[...] = small_mm(start_value[...], w_out[...])
+            for i in range(2, 5):
+                lift(i).start()
 
         def relay(b):
             here = block_rows(b)
+
             total = None
             for group in groups:
                 for c in group:
@@ -287,11 +363,11 @@
                 mean = jnp.sum(v_rows.astype(F32) * values_wide[here, :], axis=-1, keepdims=True) * (1.0 / dw)
                 pass_on(b, mean, lambda cols: mm(v_rows, w_value_t[:, cols]))
 
-            @pl.when(section == 0)
-            def _():
-                add_block(here)
-
         each_block(relay)
+
+        @pl.when(section == last - 1)
+        def _():
+            error_parts()
 
     def packed(x):
         return jnp.concatenate([x[:, :LANES], x[:, LANES:]], axis=0).astype(BF16)
@@ -302,8 +378,8 @@
     def far_first(k):
         return lax.rem(chip + chips // 2 + 2 + k, chips)
 
-    def exchange(part, seen, total, phase, meanwhile, finish):
-        def scatter(k, carry):
+    def scatter(part, seen, phase):
+        def body(k, carry):
             to = far_first(k)
 
             @pl.when((to < tiles) & ((to != chip) | (core == 0)))
@@ -319,38 +395,45 @@
 
             return carry
 
-        lax.fori_loop(0, chips, scatter, 0)
-        extra = meanwhile()
-
+        lax.fori_loop(0, chips, body, 0)
+
+    def summed(part, seen, phase):
+        seen[me] = part[chip]
+        arrivals(seen, replicas - 1, reduce_recv.at[2 * phase]).wait()
+        return jnp.sum(seen[...].astype(F32), axis=0)
+
+    def spread(source, total, phase, arrival, to_section, to_self):
+        def body(k, carry):
+            to = far_first(k)
+            for end in range(2):
+
+                @pl.when((to != chip) | (end == 0) | to_self)
+                def _():
+                    pltpu.make_async_remote_copy(
+                        src_ref=source.at[chip],
+                        dst_ref=total.at[chip],
+                        send_sem=reduce_send.at[2 * phase + 1],
+                        recv_sem=reduce_recv.at[arrival],
+                        device_id={"section": to_section, "dp": 2 * to + end},
+                        device_id_type=pl.DeviceIdType.MESH,
+                    ).start()
+
+            return carry
+
+        lax.fori_loop(0, chips, body, 0)
+
+    def gathered(total, phase):
         @pl.when(owner)
         def _():
-            seen[me] = part[chip]
-            arrivals(seen, replicas - 1, reduce_recv.at[2 * phase]).wait()
-            total[chip] = finish(jnp.sum(seen[...].astype(F32), axis=0), extra).astype(BF16)
-
-            def spread(k, carry):
-                to = far_first(k)
-                for end in range(2):
-
-                    @pl.when((to != chip) | (end == 0))
-                    def _():
-                        pltpu.make_async_remote_copy(
-                            src_ref=total.at[chip],
-                            dst_ref=total.at[chip],
-                            send_sem=reduce_send.at[2 * phase + 1],
-                            recv_sem=reduce_recv.at[2 * phase + 1],
-                            device_id={"dp": 2 * to + end},
-                            device_id_type=pl.DeviceIdType.MESH,
-                        ).start()
-
-                return carry
-
-            lax.fori_loop(0, chips, spread, 0)
             arrivals(total, tiles - 1, reduce_recv.at[2 * phase + 1]).wait()
 
         @pl.when(jnp.logical_not(owner))
         def _():
             arrivals(total, tiles, reduce_recv.at[2 * phase + 1]).wait()
+
+    def pack_all(part, ref):
+        for j in range(tiles):
+            ref[j] = packed(part[:, 2 * LANES * j : 2 * LANES * (j + 1)])
 
     def finish_sends(seen, phase):
         @pl.when(owner)
@@ -362,13 +445,38 @@
         def _():
             arrivals(seen, tiles, reduce_send.at[2 * phase]).wait()
 
-    @pl.when(section > 0)
+    @pl.when(lifts)
+    def _():
+        for i in range(5):
+            lift(i).wait_recv()
+        add_lower(slice(None))
+
+        pack_all(lower_part, lower_packed)
+        scatter(lower_packed, lower_seen, 2)
+
+    @pl.when(jnp.logical_not(lifted))
     def _():
         add_block(slice(None))
-
-    for j in range(tiles):
-        p_packed[j] = packed(p_part[:, 2 * LANES * j : 2 * LANES * (j + 1)])
-    exchange(p_packed, p_seen, p_total, 0, lambda: None, lambda tile, extra: tile)
+        pack_all(p_part, p_packed)
+        scatter(p_packed, p_seen, 0)
+
+    @pl.when(lifts & owner)
+    def _():
+        lower_total[chip] = summed(lower_packed, lower_seen, 2).astype(BF16)
+        spread(lower_total, p_total, 2, 1, section - 1, True)
+
+    @pl.when(jnp.logical_not(lifted) & owner)
+    def _():
+        p_total[chip] = summed(p_packed, p_seen, 0).astype(BF16)
+        spread(p_total, p_total, 0, 1, section, False)
+
+    @pl.when(jnp.logical_not(lifted))
+    def _():
+        gathered(p_total, 0)
+
+    @pl.when(lifted)
+    def _():
+        arrivals(p_total, tiles, reduce_recv.at[1]).wait()
 
     def unpacked(first, count):
         halves = [p_total[j] for j in range(first, first + count)]
@@ -400,10 +508,32 @@
         lower = jnp.where(chip < out_tiles, for_value, for_out)
         return jnp.concatenate([apply_small(lower, pair[:8]), apply_small(lower, pair[8:])], axis=0)
 
-    exchange(q_packed, q_seen, q_total, 1, factors, solved)
+    scatter(q_packed, q_seen, 1)
+    extra = factors()
+
+    @pl.when(owner)
+    def _():
+        q_total[chip] = solved(summed(q_packed, q_seen, 1), extra).astype(BF16)
+        spread(q_total, q_total, 1, 3, section, False)
+
+    gathered(q_total, 1)
     out_ref[...] = q_total[...]
-    finish_sends(p_seen, 0)
     finish_sends(q_seen, 1)
+
+    @pl.when(jnp.logical_not(lifted))
+    def _():
+        finish_sends(p_seen, 0)
+
+    @pl.when(lifts)
+    def _():
+        @pl.when(owner)
+        def _():
+            arrivals(lower_seen, tiles - 1, reduce_send.at[4]).wait()
+            arrivals(lower_seen, replicas, reduce_send.at[5]).wait()
+
+        @pl.when(jnp.logical_not(owner))
+        def _():
+            arrivals(lower_seen, tiles, reduce_send.at[4]).wait()
 
     @pl.when(section > 0)
     def _():
@@ -412,6 +542,11 @@
                 hop(b, c).wait_send()
 
         each_block(sent)
+
+    @pl.when(lifted)
+    def _():
+        for i in range(5):
+            lift(i).wait_send()
 
 
 def part_kernel(both, out_value, out_out):
@@ -474,8 +609,19 @@
                 pltpu.SemaphoreType.DMA((9,)),
                 pltpu.SemaphoreType.DMA((blocks * (len(cuts) - 1),)),
                 pltpu.SemaphoreType.DMA((blocks * (len(cuts) - 1),)),
-                pltpu.SemaphoreType.DMA((4,)),
-                pltpu.SemaphoreType.DMA((4,)),
+                pltpu.SemaphoreType.DMA((6,)),
+                pltpu.SemaphoreType.DMA((6,)),
+                pltpu.VMEM((rows, dw), BF16),
+                pltpu.VMEM((rows, hv), BF16),
+                pltpu.VMEM((rank, dw), F32),
+                pltpu.VMEM((rank, dw), F32),
+                pltpu.VMEM((rank, dw + hv), F32),
+                pltpu.VMEM((tiles, 2 * rank, LANES), BF16),
+                pltpu.VMEM((replicas, 2 * rank, LANES), BF16),
+                pltpu.VMEM((tiles, 2 * rank, LANES), BF16),
+                pltpu.VMEM((rank, dw), F32),
+                pltpu.SemaphoreType.DMA((5,)),
+                pltpu.SemaphoreType.DMA((5,)),
             ],
             compiler_params=pltpu.CompilerParams(
                 collective_id=0, has_side_effects=True, vmem_limit_bytes=60 * 2**20

time: 77.2 us -> 75.7 us (0.981)
  Pallas kernels: 75.1 us -> 73.6 us
    pallas_call x1, Pallas kernels: 73.7 us -> 72.2 us  [shards(): pl.pallas_call(functools.partial(kernel, sections, replicas, blocks, cuts...]
where the time goes in v3:
time: 75.7 us; the launch traced here: 75.5 us
  Pallas kernels  73.6 us (97%)
  between operations  1.29 us (2%)
    pallas_call x1, Pallas kernels, shards(): pl.pallas_call(functools.partial(kernel, sections, replicas, blocks, cuts...  72.2 us

profile of v3, /device:TPU:1, one launch (start us, length us, event | category | flops | bytes accessed | tf_op | source)
XLA Modules:
  0.0 75.5 jit_solution(8113383435278615181)
XLA Ops:
  1.3 72.2 %shard_map.113.both = bf16[12,16,128]{2,1,0:T(8,128)(2,1)S(1)} custom-call(bf16[128,2560]{1,0:T(8,128)(2,1)} %bitcast.21, bf16[128,2560]{1,0:T(8,128)(2,1)} %top_hbm.1, s32[1]{0:T(128)S(6)} %copy.12.count_ref, f32[1,2560]{1,0:T(1,128)} %gain_hbm.1, bf16[2560,512]{1,0:T(8,128)(2,1)} %bitcast.17, bf16[512,2560]{1,0:T(8,128)(2,1)} %bitcast.18, ...), custom_call_target="tpu_custom_call" | custom-call | flops 1700000000 | bytes 12000000 | tf_op jit(solution)/shard_map/pallas_call | solution.py:575
  73.5 0.0 copy-start
  73.5 0.6 copy-done
  74.1 1.4 %shard_map.114 = (f32[8,512]{1,0:T(8,128)}, f32[8,2560]{1,0:T(8,128)}) custom-call(bf16[12,16,128]{2,1,0:T(8,128)(2,1)} %copy-done), custom_call_target="tpu_custom_call" | custom-call | tf_op jit(solution)/shard_map/pallas_call | solution.py:642
Async XLA Ops:
  73.5 0.6 copy-start

commit v4 on v3

--- a/solution.py
+++ b/solution.py
@@ -1,4 +1,5 @@
 import functools
+import math
 
 import jax
 import jax.numpy as jnp
@@ -79,7 +80,8 @@
     err_out_hbm,
     q_value_hbm,
     q_out_hbm,
-    out_ref,
+    out_value,
+    out_out,
     acts,
     top,
     gain,
@@ -122,6 +124,7 @@
     lower_seen,
     lower_total,
     value_q,
+    normed_t,
     lift_send,
     lift_recv,
 ):
@@ -282,6 +285,7 @@
         wide = mm(normed[...], w_value[...])
         values_wide[...] = wide
         values[...] = wide.astype(BF16)
+        normed_t[...] = normed[...].T
 
     @pl.when(section == last)
     def _():
@@ -375,14 +379,22 @@
     def arrivals(ref, amount, sem):
         return pltpu.make_async_copy(ref.at[pl.ds(0, amount)], ref.at[pl.ds(0, amount)], sem)
 
-    def far_first(k):
-        return lax.rem(chip + chips // 2 + 2 + k, chips)
+    side = math.isqrt(chips) if math.isqrt(chips) ** 2 == chips else 1
+    height = chips // side
+
+    def hops(offset):
+        return min(offset[0], height - offset[0]) + min(offset[1], side - offset[1])
+
+    offsets = sorted(((dy, dx) for dy in range(height) for dx in range(side)), key=hops, reverse=True)
+    farthest_first = [
+        (hops(o) == 0, lax.rem(chip // side + o[0], height) * side + lax.rem(lax.rem(chip, side) + o[1], side))
+        for o in offsets
+    ]
 
     def scatter(part, seen, phase):
-        def body(k, carry):
-            to = far_first(k)
-
-            @pl.when((to < tiles) & ((to != chip) | (core == 0)))
+        for here, to in farthest_first:
+
+            @pl.when((to < tiles) & (core == 0) if here else to < tiles)
             def _():
                 pltpu.make_async_remote_copy(
                     src_ref=part.at[to],
@@ -393,34 +405,22 @@
                     device_id_type=pl.DeviceIdType.MESH,
                 ).start()
 
-            return carry
-
-        lax.fori_loop(0, chips, body, 0)
-
     def summed(part, seen, phase):
         seen[me] = part[chip]
         arrivals(seen, replicas - 1, reduce_recv.at[2 * phase]).wait()
         return jnp.sum(seen[...].astype(F32), axis=0)
 
     def spread(source, total, phase, arrival, to_section, to_self):
-        def body(k, carry):
-            to = far_first(k)
-            for end in range(2):
-
-                @pl.when((to != chip) | (end == 0) | to_self)
-                def _():
-                    pltpu.make_async_remote_copy(
-                        src_ref=source.at[chip],
-                        dst_ref=total.at[chip],
-                        send_sem=reduce_send.at[2 * phase + 1],
-                        recv_sem=reduce_recv.at[arrival],
-                        device_id={"section": to_section, "dp": 2 * to + end},
-                        device_id_type=pl.DeviceIdType.MESH,
-                    ).start()
-
-            return carry
-
-        lax.fori_loop(0, chips, body, 0)
+        for here, to in farthest_first:
+            for end in range(1 if here and not to_self else 2):
+                pltpu.make_async_remote_copy(
+                    src_ref=source.at[chip],
+                    dst_ref=total.at[chip],
+                    send_sem=reduce_send.at[2 * phase + 1],
+                    recv_sem=reduce_recv.at[arrival],
+                    device_id={"section": to_section, "dp": 2 * to + end},
+                    device_id_type=pl.DeviceIdType.MESH,
+                ).start()
 
     def gathered(total, phase):
         @pl.when(owner)
@@ -487,7 +487,7 @@
     p_all[:, :dw] = p_value
     p_all[:, dw:] = p_out
     p_value, p_out = p_value.astype(BF16), p_out.astype(BF16)
-    q_value = small_mm(mm_nt(p_value, normed[...]) * scale, value_grad[...]) + mm(p_value, err_value[...])
+    q_value = small_mm(mm(p_value, normed_t[...]) * scale, value_grad[...]) + mm(p_value, err_value[...])
     for j in range(out_tiles):
         q_packed[j] = packed(q_value[:, 2 * LANES * j : 2 * LANES * (j + 1)])
     q_out = small_mm(mm_nt(p_out, values[...]) * scale, grads[...]) + mm(p_out, err_out[...])
@@ -517,7 +517,11 @@
         spread(q_total, q_total, 1, 3, section, False)
 
     gathered(q_total, 1)
-    out_ref[...] = q_total[...]
+    for j in range(tiles):
+        ref, place = (out_value, j) if j < out_tiles else (out_out, j - out_tiles)
+        tile = q_total[j].astype(F32)
+        ref[:, 2 * LANES * place : 2 * LANES * place + LANES] = tile[:8]
+        ref[:, 2 * LANES * place + LANES : 2 * LANES * (place + 1)] = tile[8:]
     finish_sends(q_seen, 1)
 
     @pl.when(jnp.logical_not(lifted))
@@ -547,16 +551,6 @@
     def _():
         for i in range(5):
             lift(i).wait_send()
-
-
-def part_kernel(both, out_value, out_out):
-    out_tiles = out_value.shape[1] // (2 * LANES)
-    for j in range(both.shape[0]):
-        ref, place = (out_value, j) if j < out_tiles else (out_out, j - out_tiles)
-        tile = both[j].astype(F32)
-        half = tile.shape[0] // 2
-        ref[:, 2 * LANES * place : 2 * LANES * place + LANES] = tile[:half]
-        ref[:, 2 * LANES * place + LANES : 2 * LANES * (place + 1)] = tile[half:]
 
 
 def solution(mesh):
@@ -572,11 +566,11 @@
         cuts = tuple(cut * dw // CUTS[-1] for cut in CUTS)
         any_space = pl.BlockSpec(memory_space=pl.ANY)
         vmem = pl.BlockSpec(memory_space=pltpu.VMEM)
-        both = pl.pallas_call(
+        q_value, q_out = pl.pallas_call(
             functools.partial(kernel, sections, replicas, blocks, cuts, GROUPS),
-            out_shape=pltpu.VMEM((tiles, 2 * rank, LANES), BF16),
+            out_shape=(pltpu.VMEM((rank, hv), F32), pltpu.VMEM((rank, dw), F32)),
             in_specs=[any_space] * 2 + [pl.BlockSpec(memory_space=pltpu.SMEM)] + [any_space] * 7,
-            out_specs=vmem,
+            out_specs=(vmem, vmem),
             scratch_shapes=[
                 pltpu.VMEM((rows, dw), BF16),
                 pltpu.VMEM((rows, dw), BF16),
@@ -620,6 +614,7 @@
                 pltpu.VMEM((replicas, 2 * rank, LANES), BF16),
                 pltpu.VMEM((tiles, 2 * rank, LANES), BF16),
                 pltpu.VMEM((rank, dw), F32),
+                pltpu.VMEM((dw, rows), BF16),
                 pltpu.SemaphoreType.DMA((5,)),
                 pltpu.SemaphoreType.DMA((5,)),
             ],
@@ -639,15 +634,6 @@
             start_q_value[0].T,
             start_q_out[0].T,
         )
-        q_value, q_out = pl.pallas_call(
-            part_kernel,
-            out_shape=(
-                jax.ShapeDtypeStruct((rank, hv), F32),
-                jax.ShapeDtypeStruct((rank, dw), F32),
-            ),
-            in_specs=[vmem],
-            out_specs=(vmem, vmem),
-        )(both)
         return q_value.T[None], q_out.T[None]
 
     placed = (

time: 75.7 us -> 73.3 us (0.968)
  Pallas kernels: 73.6 us -> 70.7 us
    pallas_call x1, Pallas kernels: 72.2 us -> 70.7 us  [shards(): pl.pallas_call(functools.partial(kernel, sections, replicas, blocks, cuts...]
    pallas_call x1 -> x0, Pallas kernels: 1.44 us -> none  [shards(): pl.pallas_call(part_kernel, out_shape=(jax.ShapeDtypeStruct((rank, hv), F...]
where the time goes in v4:
time: 73.3 us; the launch traced here: 73.2 us
  Pallas kernels  70.7 us (96%)
  between operations  1.29 us (2%)
  local copies, waits for them, and re-layouts  1.24 us (2%)
    pallas_call x1, Pallas kernels, shards(): pl.pallas_call(functools.partial(kernel, sections, replicas, blocks, cuts...  70.7 us

profile of v4, /device:TPU:1, one launch (start us, length us, event | category | flops | bytes accessed | tf_op | source)
XLA Modules:
  0.0 73.2 jit_solution(4309454515051514278)
XLA Ops:
  1.3 70.7 %shard_map.113 = (f32[8,512]{1,0:T(8,128)S(1)}, f32[8,2560]{1,0:T(8,128)S(1)}) custom-call(bf16[128,2560]{1,0:T(8,128)(2,1)} %bitcast.23, bf16[128,2560]{1,0:T(8,128)(2,1)} %top_hbm.1, s32[1]{0:T(128)S(6)} %copy.16.count_ref, f32[1,2560]{1,0:T(1,128)} %gain_hbm.1, bf16[2560,512]{1,0:T(8,128)(2,1)} %bitcast.19, bf16[512,2560]{1,0:T(8,128)(2,1)} %bitcast.20, ...), custom_call_target="tpu_custom_call" | custom-call | flops 1700000000 | bytes 12000000 | tf_op jit(solution)/shard_map/pallas_call | solution.py:569
  72.0 0.6 copy.14
  72.6 0.6 copy.15

commit v5 on v4

--- a/solution.py
+++ b/solution.py
@@ -160,7 +160,7 @@
         )
     ]
     (l_top, l_w_out, l_acts, l_gain, l_w_value, l_q_value, l_q_out, l_err_value, l_err_out) = loads
-    for load in loads[:4]:
+    for load in loads[:5]:
         load.start()
 
     barrier = pltpu.get_barrier_semaphore()
@@ -290,7 +290,6 @@
     @pl.when(section == last)
     def _():
         l_top.wait()
-        l_w_value.start()
         live = lax.broadcasted_iota(jnp.int32, (rows, 1), 0) < count
         grads[...] = jnp.where(live, top[...].astype(F32), 0.0).astype(BF16)
         l_w_out.wait()
@@ -318,7 +317,6 @@
     @pl.when(section < last)
     def _():
         l_acts.wait()
-        l_w_value.start()
         l_gain.wait()
         for load in loads[5:]:
             load.start()
@@ -391,10 +389,12 @@
         for o in offsets
     ]
 
-    def scatter(part, seen, phase):
+    def scatter(part, seen, phase, first, end):
         for here, to in farthest_first:
 
-            @pl.when((to < tiles) & (core == 0) if here else to < tiles)
+            wanted = (to >= first) & (to < end)
+
+            @pl.when(wanted & (core == 0) if here else wanted)
             def _():
                 pltpu.make_async_remote_copy(
                     src_ref=part.at[to],
@@ -452,13 +452,13 @@
         add_lower(slice(None))
 
         pack_all(lower_part, lower_packed)
-        scatter(lower_packed, lower_seen, 2)
+        scatter(lower_packed, lower_seen, 2, 0, tiles)
 
     @pl.when(jnp.logical_not(lifted))
     def _():
         add_block(slice(None))
         pack_all(p_part, p_packed)
-        scatter(p_packed, p_seen, 0)
+        scatter(p_packed, p_seen, 0, 0, tiles)
 
     @pl.when(lifts & owner)
     def _():
@@ -487,12 +487,14 @@
     p_all[:, :dw] = p_value
     p_all[:, dw:] = p_out
     p_value, p_out = p_value.astype(BF16), p_out.astype(BF16)
+    q_out = small_mm(mm_nt(p_out, values[...]) * scale, grads[...]) + mm(p_out, err_out[...])
+    for j in range(value_tiles):
+        q_packed[out_tiles + j] = packed(q_out[:, 2 * LANES * j : 2 * LANES * (j + 1)])
+    scatter(q_packed, q_seen, 1, out_tiles, tiles)
     q_value = small_mm(mm(p_value, normed_t[...]) * scale, value_grad[...]) + mm(p_value, err_value[...])
     for j in range(out_tiles):
         q_packed[j] = packed(q_value[:, 2 * LANES * j : 2 * LANES * (j + 1)])
-    q_out = small_mm(mm_nt(p_out, values[...]) * scale, grads[...]) + mm(p_out, err_out[...])
-    for j in range(value_tiles):
-        q_packed[out_tiles + j] = packed(q_out[:, 2 * LANES * j : 2 * LANES * (j + 1)])
+    scatter(q_packed, q_seen, 1, 0, out_tiles)
 
     def factors():
         grams = [
@@ -508,7 +510,6 @@
         lower = jnp.where(chip < out_tiles, for_value, for_out)
         return jnp.concatenate([apply_small(lower, pair[:8]), apply_small(lower, pair[8:])], axis=0)
 
-    scatter(q_packed, q_seen, 1)
     extra = factors()
 
     @pl.when(owner)

time: 73.3 us -> 72.6 us (level)
  no operation moved by 1% of the time
where the time goes in v5:
time: 72.6 us
  Pallas kernels  70 us (96%)
  between operations  1.29 us (2%)
  local copies, waits for them, and re-layouts  1.24 us (2%)
    pallas_call x1, Pallas kernels, shards(): pl.pallas_call(functools.partial(kernel, sections, replicas, blocks, cuts...  70 us

profile of v5, /device:TPU:1, one launch (start us, length us, event | category | flops | bytes accessed | tf_op | source)
XLA Modules:
  0.0 72.6 jit_solution(12761891920112956710)
XLA Ops:
  1.3 70.0 %shard_map.113 = (f32[8,512]{1,0:T(8,128)S(1)}, f32[8,2560]{1,0:T(8,128)S(1)}) custom-call(bf16[128,2560]{1,0:T(8,128)(2,1)} %bitcast.23, bf16[128,2560]{1,0:T(8,128)(2,1)} %top_hbm.1, s32[1]{0:T(128)S(6)} %copy.16.count_ref, f32[1,2560]{1,0:T(1,128)} %gain_hbm.1, bf16[2560,512]{1,0:T(8,128)(2,1)} %bitcast.19, bf16[512,2560]{1,0:T(8,128)(2,1)} %bitcast.20, ...), custom_call_target="tpu_custom_call" | custom-call | flops 1700000000 | bytes 12000000 | tf_op jit(solution)/shard_map/pallas_call | solution.py:570
  71.3 0.6 copy.14
  71.9 0.6 copy.15

commit v6 on v5

--- a/solution.py
+++ b/solution.py
@@ -232,11 +232,20 @@
         p_part[:, :dw] += small_mm(small_mm_nt(start_value[...], value_grad[here, :]) * scale, normed[here, :])
         p_part[:, dw:] += small_mm(small_mm_nt(start_out[...], grads[here, :]) * scale, values[here, :])
 
-    def add_lower(here):
-        along = small_mm_nt(lower_value_q[...], passed[here, :]) * scale
-        lower_part[:, :dw] += small_mm(along, lower_normed[here, :])
-        along = small_mm_nt(lower_out_q[...], passed[here, :]) * scale
-        lower_part[:, dw:] += small_mm(along, lower_values[here, :])
+    def pack_some(part, ref, first, end):
+        for j in range(first, end):
+            ref[j] = packed(part[:, 2 * LANES * j : 2 * LANES * (j + 1)])
+
+    def lower_sums():
+        factors_below = jnp.concatenate([lower_value_q[...], lower_out_q[...]], axis=0)
+        along = small_mm_nt(factors_below, passed[...]) * scale
+        rank = lower_part.shape[0]
+        lower_part[:, :dw] += small_mm(along[:rank], lower_normed[...])
+        pack_some(lower_part, lower_packed, 0, value_tiles)
+        scatter(lower_packed, lower_seen, 2, 0, value_tiles)
+        lower_part[:, dw:] += small_mm(along[rank:], lower_values[...])
+        pack_some(lower_part, lower_packed, value_tiles, tiles)
+        scatter(lower_packed, lower_seen, 2, value_tiles, tiles)
 
     def lift(i):
         src, dst = [
@@ -431,10 +440,6 @@
         def _():
             arrivals(total, tiles, reduce_recv.at[2 * phase + 1]).wait()
 
-    def pack_all(part, ref):
-        for j in range(tiles):
-            ref[j] = packed(part[:, 2 * LANES * j : 2 * LANES * (j + 1)])
-
     def finish_sends(seen, phase):
         @pl.when(owner)
         def _():
@@ -449,15 +454,13 @@
     def _():
         for i in range(5):
             lift(i).wait_recv()
-        add_lower(slice(None))
-
-        pack_all(lower_part, lower_packed)
-        scatter(lower_packed, lower_seen, 2, 0, tiles)
+        lower_sums()
+
 
     @pl.when(jnp.logical_not(lifted))
     def _():
         add_block(slice(None))
-        pack_all(p_part, p_packed)
+        pack_some(p_part, p_packed, 0, tiles)
         scatter(p_packed, p_seen, 0, 0, tiles)
 
     @pl.when(lifts & owner)

time: 72.6 us -> 72.4 us (level)
  no operation moved by 1% of the time
where the time goes in v6:
time: 72.4 us; the launch traced here: 72.3 us
  Pallas kernels  69.8 us (96%)
  between operations  1.29 us (2%)
  local copies, waits for them, and re-layouts  1.24 us (2%)
    pallas_call x1, Pallas kernels, shards(): pl.pallas_call(functools.partial(kernel, sections, replicas, blocks, cuts...  69.8 us

profile of v6, /device:TPU:1, one launch (start us, length us, event | category | flops | bytes accessed | tf_op | source)
XLA Modules:
  0.0 72.3 jit_solution(3615670744501477713)
XLA Ops:
  1.3 69.8 %shard_map.113 = (f32[8,512]{1,0:T(8,128)S(1)}, f32[8,2560]{1,0:T(8,128)S(1)}) custom-call(bf16[128,2560]{1,0:T(8,128)(2,1)} %bitcast.23, bf16[128,2560]{1,0:T(8,128)(2,1)} %top_hbm.1, s32[1]{0:T(128)S(6)} %copy.16.count_ref, f32[1,2560]{1,0:T(1,128)} %gain_hbm.1, bf16[2560,512]{1,0:T(8,128)(2,1)} %bitcast.19, bf16[512,2560]{1,0:T(8,128)(2,1)} %bitcast.20, ...), custom_call_target="tpu_custom_call" | custom-call | flops 1700000000 | bytes 12000000 | tf_op jit(solution)/shard_map/pallas_call | solution.py:573
  71.1 0.6 copy.14
  71.7 0.6 copy.15

commit v7 on v6

--- a/solution.py
+++ b/solution.py
@@ -10,7 +10,7 @@
 
 EPSILON = 1e-06
 LANES = 128
-CUTS = (0, 5, 10, 15, 20)
+CUTS = (0, 6, 12, 17, 20)
 GROUPS = ((0,), (1,), (2,), (3,))
 LIFTED = 2
 BF16 = jnp.bfloat16

time: 72.4 us -> 72.4 us (level)
  no operation moved by 1% of the time
where the time goes in v7:
time: 72.4 us; the launch traced here: 72.3 us
  Pallas kernels  69.7 us (96%)
  between operations  1.29 us (2%)
  local copies, waits for them, and re-layouts  1.24 us (2%)
    pallas_call x1, Pallas kernels, shards(): pl.pallas_call(functools.partial(kernel, sections, replicas, blocks, cuts...  69.7 us

profile of v7, /device:TPU:1, one launch (start us, length us, event | category | flops | bytes accessed | tf_op | source)
XLA Modules:
  0.0 72.3 jit_solution(5791294091287566757)
XLA Ops:
  1.3 69.7 %shard_map.113 = (f32[8,512]{1,0:T(8,128)S(1)}, f32[8,2560]{1,0:T(8,128)S(1)}) custom-call(bf16[128,2560]{1,0:T(8,128)(2,1)} %bitcast.23, bf16[128,2560]{1,0:T(8,128)(2,1)} %top_hbm.1, s32[1]{0:T(128)S(6)} %copy.16.count_ref, f32[1,2560]{1,0:T(1,128)} %gain_hbm.1, bf16[2560,512]{1,0:T(8,128)(2,1)} %bitcast.19, bf16[512,2560]{1,0:T(8,128)(2,1)} %bitcast.20, ...), custom_call_target="tpu_custom_call" | custom-call | flops 1700000000 | bytes 12000000 | tf_op jit(solution)/shard_map/pallas_call | solution.py:573
  71.0 0.6 copy.14
  71.6 0.6 copy.15
